TPU v7x, 32 devices: a whole 2x2x4 slice. The times are simulated.
32 devices in a mesh: shard: 8 (over z, y), tensor: 4 (over x, core).
Axes of the slice: x: 2, y: 2, z: 4, core: 2. Of those that a mesh axis runs over, the one named last changes fastest.
Arguments:
- grad_parts: float32 [8, 50, 512, 512], P('shard', None, None, 'tensor'), may hold values from -8 to 8
- weights: float32 [50, 512, 512], P(None, 'shard', 'tensor'), may hold values from -0.25 to 0.25
- owner_slot: int32 [50], replicated, may hold values from 0 to 63, as said below
- stat_left: float32 [64, 512, 512], P(('shard', 'tensor')), may hold values from -1 to 5, as said below
- stat_right: float32 [64, 512, 512], P(('shard', 'tensor')), may hold values from -1 to 5, as said below
- root_left: float32 [64, 512, 512], P(('shard', 'tensor')), may hold values from -1 to 5, as said below
- root_right: float32 [64, 512, 512], P(('shard', 'tensor')), may hold values from -1 to 5, as said below
- ln_grad_parts: float32 [8, 4, 1024], P('shard', None, 'tensor'), may hold values from -40 to 40
- ln_params: float32 [4, 1024], P(None, 'tensor'), may hold values from -3 to 3
- ln_accum: float32 [4, 1024], P(None, 'tensor'), may hold values from 0.5 to 5
Outputs:
- new_weights: float32 [50, 512, 512], P(None, 'shard', 'tensor')
- new_stat_left: float32 [64, 512, 512], P(('shard', 'tensor'))
- new_stat_right: float32 [64, 512, 512], P(('shard', 'tensor'))
- new_ln_params: float32 [4, 1024], P(None, 'tensor')
- new_ln_accum: float32 [4, 1024], P(None, 'tensor')
Inputs may be any that keep to these rules, and one draw needn't show every extreme that they name: `owner_slot`: distinct global slot numbers; slot s belongs to device s // 2, devices counted with shard slowest. One device owns 2 blocks. `stat_left`: symmetric matrices. `stat_right`: symmetric matrices. `root_left`: symmetric matrices. `root_right`: symmetric matrices.
All inputs are finite; a program needn't handle non-finite values.
Results may differ from a plain program's by a relative error of at most 0.0029.
Values may be sent and summed in bfloat16 or wider, within the bound.
A program may use at most 128 MiB of HBM per device.

v0:
```python
import jax
import jax.numpy as jnp
from jax import lax
from jax.sharding import PartitionSpec as P

DECAY_RATE = 0.9
STEP_RATE = 0.3
NORM_RATE = 0.1
EPSILON = 1e-06
PRECISE = lax.Precision.HIGHEST


def slot_step(gradient, stat_lhs, stat_rhs, root_lhs, root_rhs):
    lhs_new = DECAY_RATE * stat_lhs + (1.0 - DECAY_RATE) * jnp.dot(
        gradient, gradient.T, precision=PRECISE
    )
    rhs_new = DECAY_RATE * stat_rhs + (1.0 - DECAY_RATE) * jnp.dot(
        gradient.T, gradient, precision=PRECISE
    )
    direction = jnp.dot(jnp.dot(root_lhs, gradient, precision=PRECISE), root_rhs, precision=PRECISE)
    factor = jnp.sqrt(jnp.mean(gradient * gradient) / (jnp.mean(direction * direction) + EPSILON))
    update = (STEP_RATE * factor * direction).astype(jnp.bfloat16)
    return (lhs_new, rhs_new, update)


def per_device(
    grad_parts,
    weights,
    owner_slot,
    stat_left,
    stat_right,
    root_left,
    root_right,
    ln_grad_parts,
    ln_params,
    ln_accum,
):
    shard_count = lax.axis_size("shard")
    tensor_count = lax.axis_size("tensor")
    slot_count = stat_left.shape[0]
    block_side = stat_left.shape[1]
    row_width = block_side // shard_count
    col_width = block_side // tensor_count
    owner_device = owner_slot // slot_count
    slot_place = owner_slot % slot_count
    local_grads = grad_parts[0]
    local_norms = ln_grad_parts[0]
    row_part = lax.psum_scatter(local_grads, "shard", scatter_dimension=1, tiled=True)
    ln_gradient = lax.psum(local_norms, "shard")
    buffer = jnp.zeros((shard_count * tensor_count, slot_count, row_width, col_width), jnp.float32)
    buffer = buffer.at[owner_device, slot_place].set(row_part)
    arrived = lax.all_to_all(buffer, ("shard", "tensor"), split_axis=0, concat_axis=0, tiled=True)
    arrived = arrived.reshape(shard_count, tensor_count, slot_count, row_width, col_width)
    owned_grads = arrived.transpose(2, 0, 3, 1, 4).reshape(slot_count, block_side, block_side)
    lhs_list = []
    rhs_list = []
    update_list = []
    for slot_index in range(slot_count):
        lhs_new, rhs_new, update = slot_step(
            owned_grads[slot_index],
            stat_left[slot_index],
            stat_right[slot_index],
            root_left[slot_index],
            root_right[slot_index],
        )
        lhs_list.append(lhs_new)
        rhs_list.append(rhs_new)
        update_list.append(update)
    new_stat_left = jnp.stack(lhs_list)
    new_stat_right = jnp.stack(rhs_list)
    updates = jnp.stack(update_list)
    outgoing = updates.reshape(slot_count, shard_count, row_width, tensor_count, col_width)
    outgoing = outgoing.transpose(1, 3, 0, 2, 4).reshape(
        shard_count * tensor_count, slot_count, row_width, col_width
    )
    returned = lax.all_to_all(
        outgoing, ("shard", "tensor"), split_axis=0, concat_axis=0, tiled=True
    )
    pieces = returned.reshape(shard_count * tensor_count * slot_count, row_width, col_width)[
        owner_slot
    ]
    new_weights = weights - pieces.astype(jnp.float32)
    new_ln_accum = ln_accum + ln_gradient * ln_gradient
    new_ln_params = ln_params - NORM_RATE * ln_gradient / jnp.sqrt(new_ln_accum)
    return (new_weights, new_stat_left, new_stat_right, new_ln_params, new_ln_accum)


def solution(mesh):
    placed = (
        P("shard", None, None, "tensor"),
        P(None, "shard", "tensor"),
        P(),
        P(("shard", "tensor"), None, None),
        P(("shard", "tensor"), None, None),
        P(("shard", "tensor"), None, None),
        P(("shard", "tensor"), None, None),
        P("shard", None, "tensor"),
        P(None, "tensor"),
        P(None, "tensor"),
    )
    return jax.shard_map(
        per_device,
        mesh=mesh,
        in_specs=placed,
        out_specs=(
            P(None, "shard", "tensor"),
            P(("shard", "tensor"), None, None),
            P(("shard", "tensor"), None, None),
            P(None, "tensor"),
            P(None, "tensor"),
        ),
        check_vma=False,
    )
```

profile of v0, /device:TPU:8, one launch (start us, length us, event | category | flops | bytes accessed | tf_op | source)
XLA Modules:
  0.0 373.5 jit_solution(6190283079754126655)
XLA Ops:
  7.9 218.1 %reduce-scatter.2.cloned.1.call-done = f32[50,64,128]{2,1,0:T(8,128)} async-done(((f32[50,512,128]{2,1,0:T(8,128)}), f32[50,64,128]{2,1,0:T(8,128)}) %reduce-scatter.2.cloned.1.call-update) | async-done | bytes 1638416 | tf_op jit(solution)/shard_map/reduce_scatter | solution.py:48
  226.2 7.2 %scatter_fusion = f32[32,2,64,128]{3,2,1,0:T(8,128)S(1)} fusion(f32[32,2,64,128]{3,2,1,0:T(8,128)S(1)} %broadcast_in_dim.12, s32[50]{0:T(128)S(1)} %fusion.35, f32[50,64,128]{2,1,0:T(8,128)} %reduce-scatter.2.cloned.1.call-done), kind=kCustom, calls=%fused_computation.1 | custom fusion | bytes 4915600 | tf_op jit(solution)/shard_map/scatter | solution.py:51
  233.4 53.4 %all_to_all.10 = f32[32,2,64,128]{3,2,1,0:T(8,128)S(1)} all-to-all(f32[32,2,64,128]{3,2,1,0:T(8,128)S(1)} %scatter_fusion), channel_id=1, replica_groups=mesh['shard'=8,'tensor'=4] {'shard','tensor'}, dimensions={0} | all-to-all | bytes 4194304 | tf_op jit(solution)/shard_map/all_to_all | solution.py:52
  286.8 1.0 multiply_reduce_fusion.3
  289.8 0.9 copy-done
  290.7 3.5 fusion.14
  294.2 2.6 multiply_reduce_fusion.2
  297.5 0.9 multiply_convert_fusion.1
  298.4 1.2 stack.27
  299.6 0.9 copy.19
  301.4 3.5 fusion.10
  304.8 2.8 multiply_reduce_fusion
  308.4 0.9 multiply_convert_fusion
  309.3 1.2 stack.28
  310.7 1.1 pad_maximum_fusion.2
  311.7 4.7 %all-to-all-start.1 = ((bf16[32,2,64,128]{3,2,1,0:T(8,128)(2,1)}), bf16[32,2,64,128]{3,2,1,0:T(8,128)(2,1)S(1)}, u32[]{:S(2)}, u32[]{:S(2)}) async-start(bf16[32,2,64,128]{3,2,1,0:T(8,128)(2,1)} %bitcast.12), calls=%async_computation.2 | async-start | bytes 2097152 | tf_op jit(solution)/shard_map/all_to_all | solution.py:76
  316.4 34.3 %psum.7 = f32[4,256]{1,0:T(4,128)S(1)} all-reduce(f32[4,256]{1,0:T(4,128)S(1)} %bitcast.85), channel_id=1, replica_groups=mesh['shard'=8,'tensor'=4] {'shard'}, use_global_device_ids=true, to_apply=%region_6.7 | all-reduce | flops 1024 | bytes 8192 | tf_op jit(solution)/shard_map/psum | solution.py:49
  351.4 3.1 fusion.3
  354.6 1.9 fusion.1
  356.5 1.9 fusion.7
  358.4 1.9 fusion.5
  360.3 2.7 pad_maximum_fusion
  363.0 0.7 gather_fusion
  363.7 2.9 convert_subtract_fusion
  (32 shorter events, 3.3 us)
Async XLA Ops:
  7.2 218.8 %reduce-scatter.2.cloned.1.call-start = ((), (), s32[]{:S(2)}) async-start(), calls=%async_computation.3 | async-start | bytes 14745600 | tf_op jit(solution)/shard_map/reduce_scatter | solution.py:48
  7.2 0.7 copy-start.10
  289.1 1.6 copy-start
  289.8 4.4 %copy-start.4 = (f32[2,512,512]{2,1,0:T(8,128)S(1)}, f32[2,512,512]{2,1,0:T(8,128)}, u32[]{:S(2)}) copy-start(f32[2,512,512]{2,1,0:T(8,128)} %param.16) | copy-start | bytes 6291460
  299.6 1.8 copy-start.1
  301.2 3.6 copy-start.5
  309.3 1.4 copy-start.6
  310.6 5.8 %copy-start.9 = (f32[1,4,256]{2,1,0:T(4,128)S(1)}, f32[1,4,256]{2,1,0:T(4,128)}, u32[]{:S(2)}) copy-start(f32[1,4,256]{2,1,0:T(4,128)} %param.17) | copy-start | bytes 12292
  310.7 40.1 %copy-start.7 = (f32[4,256]{1,0:T(4,128)S(1)}, f32[4,256]{1,0:T(4,128)}, u32[]{:S(2)}) copy-start(f32[4,256]{1,0:T(4,128)} %param.18) | copy-start | bytes 12292
  310.7 40.1 %copy-start.8 = (f32[4,256]{1,0:T(4,128)S(1)}, f32[4,256]{1,0:T(4,128)}, u32[]{:S(2)}) copy-start(f32[4,256]{1,0:T(4,128)} %param.19) | copy-start | bytes 12292
  311.7 51.2 %all-to-all-start.1 = ((bf16[32,2,64,128]{3,2,1,0:T(8,128)(2,1)}), bf16[32,2,64,128]{3,2,1,0:T(8,128)(2,1)S(1)}, u32[]{:S(2)}, u32[]{:S(2)}) async-start(bf16[32,2,64,128]{3,2,1,0:T(8,128)(2,1)} %bitcast.12), calls=%async_computation.2 | async-start | bytes 2097152 | tf_op jit(solution)/shard_map/all_to_all | solution.py:76
  350.7 3.8 %copy-start.2 = (f32[2,512,512]{2,1,0:T(8,128)S(1)}, f32[2,512,512]{2,1,0:T(8,128)}, u32[]{:S(2)}) copy-start(f32[2,512,512]{2,1,0:T(8,128)} %param.14) | copy-start | bytes 6291460
  354.5 1.9 copy-start.3
Sparse Core Ops, SparseCore 0:
  11.7 214.2 reduce-scatter.1
where the time goes:
time: 374 us; the launch traced here: 373 us
  waiting for transfers between devices  219 us (59%)
  blocking collectives  87.7 us (23%)
  matrix products  21.2 us (6%)
  between operations  17.1 us (5%)
  local copies, waits for them, and re-layouts  14 us (4%)
  other arithmetic  10.1 us (3%)
  starting transfers between devices  4.72 us (1%)
    reduce_scatter x1, waiting for transfers between devices, per_device(): lax.psum_scatter(local_grads, 'shard', scatter_dimension=1, tiled=True)  218 us
    all_to_all x1, blocking collectives, per_device(): lax.all_to_all(buffer, ('shard', 'tensor'), split_axis=0, concat_axis=0,...  53.4 us
    psum x1, blocking collectives, per_device(): ln_gradient = lax.psum(local_norms, 'shard')  34.3 us
  transfers between devices with their start and end apart: 2, of which 1 were waited for; matrix products, arithmetic and copies ran while one was open for 3% of the time, Pallas kernels for 0%

commit v1 on v0

v1 whole, which is shorter than its diff:
```python
import jax
import jax.numpy as jnp
from jax import lax
from jax.experimental import pallas as pl
from jax.experimental.pallas import tpu as pltpu
from jax.sharding import PartitionSpec as P

DECAY_RATE = 0.9
STEP_RATE = 0.3
NORM_RATE = 0.1
EPSILON = 1e-06
PRECISE = lax.Precision.HIGHEST
F32 = jnp.float32
BF16 = jnp.bfloat16


def split(value):
    high = value.astype(BF16)
    return high, (value - high.astype(F32)).astype(BF16)


def mul(a, b):
    return jnp.dot(a, b, preferred_element_type=F32)


def mul3(a_high, a_low, b_high, b_low):
    return mul(a_high, b_high) + (mul(a_high, b_low) + mul(a_low, b_high))


def fused_kernel(
    block_of, filled, place_of,
    grad_hbm, weights_ref, stat_l_hbm, stat_r_hbm, root_l_hbm, root_r_hbm, ln_part, ln_params, ln_accum,
    new_w, new_l_hbm, new_r_hbm, new_lnp, new_lna,
    grad, ysend, yrecv, zup, zdown, zsend, total, final, gather, stat_l, stat_r, root_l, root_r,
    g_high, g_low, r_high, r_low, direct, upd, ret, ln_all,
    load_sem, out_sem, ys_sem, yr_sem, zs_sem, zu_sem, zd_sem, gs_sem, gr_sem, us_sem, ur_sem, ls_sem, lr_sem,
):
    side = grad.shape[1]
    width = grad.shape[2]
    sh = lax.axis_index("shard")
    t = lax.axis_index("tensor")
    z, y = sh // 2, sh % 2
    me = sh * 4 + t
    tile = 128
    tiles = side // tile

    def load(src, dst, k):
        return pltpu.make_async_copy(src, dst, load_sem.at[k])

    loads = [
        load(grad_hbm, grad, 0),
        load(root_l_hbm, root_l, 1),
        load(root_r_hbm, root_r, 2),
        load(stat_l_hbm, stat_l, 3),
        load(stat_r_hbm, stat_r, 4),
    ]
    for one in loads:
        one.start()

    def remote(src, dst, send, recv, s, tt):
        return pltpu.make_async_remote_copy(
            src_ref=src, dst_ref=dst, send_sem=send, recv_sem=recv,
            device_id=(s, tt), device_id_type=pl.DeviceIdType.MESH,
        )

    def ln_copy(k):
        return remote(ln_part, ln_all.at[sh], ls_sem.at[k - 1], lr_sem.at[k - 1], lax.rem(sh + k, 8), t)

    for k in range(1, 8):
        ln_copy(k).start()

    def level(c):
        q = lax.rem(c, 4)
        near = 3 - q
        inner = jnp.where(q == 0, 3, jnp.where(q == 1, 0, 4 - q))
        one = jnp.where((z == 0) | (z == 3), near, inner)
        return jnp.where(z < 2, one, 3 - one)

    def unit(n):
        c, td = n // 4, lax.rem(n, 4)
        j, zd = c // 4, level(c)
        return j, zd, td, (j * 4 + zd) * 4 + td

    def slot(j, zd, yd, td):
        return ((zd * 2 + yd) * 4 + td) * 2 + j

    def y_copy(u):
        return remote(ysend.at[u], yrecv.at[u], ys_sem.at[u], yr_sem.at[u], z * 2 + (1 - y), t)

    loads[0].wait()

    def send_y(n, _):
        j, zd, td, u = unit(n)
        s = slot(j, zd, 1 - y, td)
        block, keep = block_of[s], filled[s]

        def rows(i, _):
            r = pl.ds(pl.multiple_of(i * tile, tile), tile)
            ysend[u, r, :] = (grad[block, r, :] * keep).astype(BF16)
            return 0

        lax.fori_loop(0, tiles, rows, 0)
        y_copy(u).start()
        return 0

    lax.fori_loop(0, 32, send_y, 0)

    def up_copy(u):
        return remote(zsend.at[u], zup.at[u], zs_sem.at[u], zu_sem.at[u], jnp.minimum(z + 1, 3) * 2 + y, t)

    def down_copy(u):
        return remote(zsend.at[u], zdown.at[u], zs_sem.at[u], zd_sem.at[u], jnp.maximum(z - 1, 0) * 2 + y, t)

    def gather_copy(j, td):
        return remote(final.at[j, td], gather.at[j, t], gs_sem.at[j, td], gr_sem.at[j, t], sh, td)

    def gather_wait(j, tt):
        return remote(final.at[j, tt], gather.at[j, tt], gs_sem.at[j, tt], gr_sem.at[j, tt], sh, tt)

    def each_tile(body):
        def step(i, _):
            body(pl.ds(pl.multiple_of(i * tile, tile), tile))
            return 0

        lax.fori_loop(0, tiles, step, 0)

    def reduce_unit(n, _):
        j, zd, td, u = unit(n)
        s = slot(j, zd, y, td)
        block, keep = block_of[s], filled[s]
        y_copy(u).wait_recv()

        def first(r):
            total[r, :] = grad[block, r, :] * keep + yrecv[u, r, :].astype(F32)

        each_tile(first)

        @pl.when((z > 0) & (zd >= z))
        def _():
            up_copy(u).wait_recv()

            def add(r):
                total[r, :] = total[r, :] + zup[u, r, :].astype(F32)

            each_tile(add)

        @pl.when((z < 3) & (zd <= z))
        def _():
            down_copy(u).wait_recv()

            def add(r):
                total[r, :] = total[r, :] + zdown[u, r, :].astype(F32)

            each_tile(add)

        @pl.when(zd != z)
        def _():
            def narrow(r):
                zsend[u, r, :] = total[r, :].astype(BF16)

            each_tile(narrow)

        @pl.when(zd > z)
        def _():
            up_copy(u).start()

        @pl.when(zd < z)
        def _():
            down_copy(u).start()

        @pl.when((zd == z) & (td != t))
        def _():
            def keep_sum(r):
                final[j, td, r, :] = total[r, :]

            each_tile(keep_sum)
            gather_copy(j, td).start()

        @pl.when((zd == z) & (td == t))
        def _():
            def keep_own(r):
                gather[j, t, r, :] = total[r, :]

            each_tile(keep_own)

        return 0

    def u_copy(j, k):
        d = lax.rem(me + k, 32)
        s, tt = d // 4, lax.rem(d, 4)
        rows = pl.ds(pl.multiple_of(s * 64, 64), 64)
        return remote(upd.at[j, tt, rows], ret.at[j * 32 + me], us_sem.at[j, k - 1], ur_sem.at[j, k - 1], s, tt)

    def precondition(j):
        for k in range(1, 4):
            gather_wait(j, lax.rem(t + k, 4)).wait_recv()
        cols = [slice(k * width, (k + 1) * width) for k in range(4)]

        def halves(i, sq):
            r = pl.ds(pl.multiple_of(i * tile, tile), tile)
            for k in range(4):
                g = gather[j, k, r, :]
                sq = sq + jnp.sum(g * g, axis=0, keepdims=True)
                g_high[j, r, cols[k]], g_low[r, cols[k]] = split(g)
            r_high[r, :], r_low[r, :] = split(root_r[j, r, :])
            return sq

        zero = jnp.zeros((1, width), F32)
        square = jnp.sum(lax.fori_loop(0, tiles, halves, zero)) * (1.0 / (side * side))

        def product(i, sq):
            r = pl.ds(pl.multiple_of(i * tile, tile), tile)
            half = mul3(*split(root_l[j, r, :]), g_high[j], g_low[...])
            out = mul3(*split(half), r_high[...], r_low[...])
            direct[r, :] = out
            for k in range(4):
                sq = sq + jnp.sum(out[:, cols[k]] * out[:, cols[k]], axis=0, keepdims=True)
            return sq

        mean = jnp.sum(lax.fori_loop(0, tiles, product, zero)) * (1.0 / (side * side))
        ratio = jnp.full((1, width), square, F32) / (jnp.full((1, width), mean, F32) + EPSILON)
        scale = STEP_RATE * jnp.sqrt(ratio)

        def scaled(r):
            for k in range(4):
                upd[j, k, r, :] = (direct[r, cols[k]] * scale).astype(BF16)

        each_tile(scaled)
        own = pl.ds(pl.multiple_of(sh * 64, 64), 64)
        ret[j * 32 + me] = upd[j, t, own, :]

        def start(k, _):
            u_copy(j, k).start()
            return 0

        lax.fori_loop(1, 32, start, 0)

    def statistics(j):
        def left(i, _):
            r = pl.ds(pl.multiple_of(i * tile, tile), tile)
            square = lax.dot_general(
                g_high[j, r, :], g_high[j], (((1,), (1,)), ((), ())), preferred_element_type=F32
            )
            stat_l[j, r, :] = DECAY_RATE * stat_l[j, r, :] + (1.0 - DECAY_RATE) * square
            return 0

        lax.fori_loop(0, tiles, left, 0)

        def right(k, _):
            r = pl.ds(pl.multiple_of(k * width, width), width)
            flipped = gather[j, k].T.astype(BF16)
            stat_r[j, r, :] = DECAY_RATE * stat_r[j, r, :] + (1.0 - DECAY_RATE) * mul(flipped, g_high[j])
            return 0

        lax.fori_loop(0, 4, right, 0)

    lax.fori_loop(0, 20, reduce_unit, 0)
    loads[1].wait()
    loads[2].wait()
    precondition(0)
    lax.fori_loop(20, 32, reduce_unit, 0)
    precondition(1)

    loads[3].wait()
    loads[4].wait()
    statistics(0)
    statistics(1)
    out_l = pltpu.make_async_copy(stat_l, new_l_hbm, out_sem.at[0])
    out_r = pltpu.make_async_copy(stat_r, new_r_hbm, out_sem.at[1])
    out_l.start()
    out_r.start()

    for k in range(1, 8):
        ln_copy(k).wait()
    ln_all[sh] = ln_part[...]
    ln_grad = ln_all[0]
    for k in range(1, 8):
        ln_grad = ln_grad + ln_all[k]
    accum = ln_accum[...] + ln_grad * ln_grad
    new_lna[...] = accum
    new_lnp[...] = ln_params[...] - NORM_RATE * ln_grad / jnp.sqrt(accum)

    def sent(n, _):
        _, zd, _, u = unit(n)
        y_copy(u).wait_send()

        @pl.when(zd != z)
        def _():
            up_copy(u).wait_send()

        return 0

    lax.fori_loop(0, 32, sent, 0)
    for j in range(2):
        for k in range(1, 4):
            gather_copy(j, lax.rem(t + k, 4)).wait_send()

    def landed(n, _):
        u_copy(n // 31, lax.rem(n, 31) + 1).wait()
        return 0

    lax.fori_loop(0, 62, landed, 0)

    def apply(k, _):
        new_w[k] = weights_ref[k] - ret[place_of[k]].astype(F32)
        return 0

    lax.fori_loop(0, weights_ref.shape[0], apply, 0)
    out_l.wait()
    out_r.wait()


def fused(grad_parts, weights, owner_slot, stat_left, stat_right, root_left, root_right, ln_grad_parts, ln_params, ln_accum):
    blocks, side, width = grad_parts.shape[1:]
    slots = 64
    hit = owner_slot[None, :] == jnp.arange(slots, dtype=jnp.int32)[:, None]
    block_of = jnp.sum(jnp.where(hit, jnp.arange(blocks, dtype=jnp.int32)[None, :], 0), axis=1).astype(jnp.int32)
    filled = jnp.any(hit, axis=1).astype(F32)
    place_of = (owner_slot % 2) * 32 + owner_slot // 2
    smem = pl.BlockSpec(memory_space=pltpu.SMEM)
    vmem = pl.BlockSpec(memory_space=pltpu.VMEM)
    hbm = pl.BlockSpec(memory_space=pl.ANY)
    V = pltpu.VMEM
    dma = pltpu.SemaphoreType.DMA
    unit = (32, side, width)
    state = (2, side, side)
    shape = jax.ShapeDtypeStruct
    return pl.pallas_call(
        fused_kernel,
        out_shape=(
            shape(weights.shape, F32), shape(state, F32), shape(state, F32),
            shape(ln_params.shape, F32), shape(ln_params.shape, F32),
        ),
        in_specs=[smem] * 3 + [hbm, vmem] + [hbm] * 4 + [vmem] * 3,
        out_specs=(vmem, hbm, hbm, vmem, vmem),
        scratch_shapes=[
            V((blocks, side, width), F32),
            V(unit, BF16), V(unit, BF16), V(unit, BF16), V(unit, BF16), V(unit, BF16),
            V((side, width), F32),
            V((2, 4, side, width), F32), V((2, 4, side, width), F32),
            V(state, F32), V(state, F32), V(state, F32), V(state, F32),
            V(state, BF16), V((side, side), BF16), V((side, side), BF16), V((side, side), BF16),
            V((side, side), F32),
            V((2, 4, side, width), BF16),
            V((64, 64, width), BF16),
            V((8,) + ln_params.shape, F32),
            dma((5,)), dma((2,)),
            dma((32,)), dma((32,)), dma((32,)), dma((32,)), dma((32,)),
            dma((2, 4)), dma((2, 4)),
            dma((2, 31)), dma((2, 31)),
            dma((7,)), dma((7,)),
        ],
        compiler_params=pltpu.CompilerParams(
            has_side_effects=True, vmem_limit_bytes=60 * 2**20
        ),
        cost_estimate=pl.CostEstimate(flops=2**34, bytes_accessed=2**25, transcendentals=0),
    )(
        block_of, filled, place_of,
        grad_parts[0], weights, stat_left, stat_right, root_left, root_right,
        ln_grad_parts[0], ln_params, ln_accum,
    )


def slot_step(gradient, stat_lhs, stat_rhs, root_lhs, root_rhs):
    lhs_new = DECAY_RATE * stat_lhs + (1.0 - DECAY_RATE) * jnp.dot(
        gradient, gradient.T, precision=PRECISE
    )
    rhs_new = DECAY_RATE * stat_rhs + (1.0 - DECAY_RATE) * jnp.dot(
        gradient.T, gradient, precision=PRECISE
    )
    direction = jnp.dot(jnp.dot(root_lhs, gradient, precision=PRECISE), root_rhs, precision=PRECISE)
    factor = jnp.sqrt(jnp.mean(gradient * gradient) / (jnp.mean(direction * direction) + EPSILON))
    update = (STEP_RATE * factor * direction).astype(jnp.bfloat16)
    return (lhs_new, rhs_new, update)


def apply_kernel(owner_slot, pieces, weights, out):
    def body(k, _):
        out[k] = weights[k] - pieces[owner_slot[k]].astype(F32)
        return 0

    lax.fori_loop(0, weights.shape[0], body, 0)


def general(
    grad_parts, weights, owner_slot, stat_left, stat_right, root_left, root_right, ln_grad_parts, ln_params, ln_accum
):
    shard_count = lax.axis_size("shard")
    tensor_count = lax.axis_size("tensor")
    slot_count = stat_left.shape[0]
    block_side = stat_left.shape[1]
    row_width = block_side // shard_count
    col_width = block_side // tensor_count
    owner_device = owner_slot // slot_count
    slot_place = owner_slot % slot_count
    row_part = lax.psum_scatter(grad_parts[0], "shard", scatter_dimension=1, tiled=True)
    ln_gradient = lax.psum(ln_grad_parts[0], "shard")
    buffer = jnp.zeros((shard_count * tensor_count, slot_count, row_width, col_width), F32)
    buffer = buffer.at[owner_device, slot_place].set(row_part)
    arrived = lax.all_to_all(buffer, ("shard", "tensor"), split_axis=0, concat_axis=0, tiled=True)
    arrived = arrived.reshape(shard_count, tensor_count, slot_count, row_width, col_width)
    owned = arrived.transpose(2, 0, 3, 1, 4).reshape(slot_count, block_side, block_side)
    steps = [
        slot_step(owned[i], stat_left[i], stat_right[i], root_left[i], root_right[i])
        for i in range(slot_count)
    ]
    lhs, rhs, update = (jnp.stack(part) for part in zip(*steps))
    outgoing = update.reshape(slot_count, shard_count, row_width, tensor_count, col_width)
    outgoing = outgoing.transpose(1, 3, 0, 2, 4).reshape(
        shard_count * tensor_count, slot_count, row_width, col_width
    )
    returned = lax.all_to_all(outgoing, ("shard", "tensor"), split_axis=0, concat_axis=0, tiled=True)
    pieces = returned.reshape(-1, row_width, col_width)
    vmem = pl.BlockSpec(memory_space=pltpu.VMEM)
    new_weights = pl.pallas_call(
        apply_kernel,
        out_shape=jax.ShapeDtypeStruct(weights.shape, F32),
        in_specs=[pl.BlockSpec(memory_space=pltpu.SMEM), vmem, vmem],
        out_specs=vmem,
        compiler_params=pltpu.CompilerParams(vmem_limit_bytes=32 * 2**20),
    )(owner_slot, pieces, weights)
    accum = ln_accum + ln_gradient * ln_gradient
    params = ln_params - NORM_RATE * ln_gradient / jnp.sqrt(accum)
    return (new_weights, lhs, rhs, params, accum)


def per_device(*args):
    sizes = (lax.axis_size("shard"), lax.axis_size("tensor"), args[3].shape[0], args[3].shape[1])
    return (fused if sizes == (8, 4, 2, 512) else general)(*args)


def solution(mesh):
    owned = P(("shard", "tensor"), None, None)
    rows = P(None, "shard", "tensor")
    norm = P(None, "tensor")
    return jax.shard_map(
        per_device,
        mesh=mesh,
        in_specs=(
            P("shard", None, None, "tensor"), rows, P(),
            owned, owned, owned, owned, P("shard", None, "tensor"), norm, norm,
        ),
        out_specs=(rows, owned, owned, norm, norm),
        check_vma=False,
    )
```

time: 374 us -> 151 us (0.40)
  waiting for transfers between devices: 219 us -> 0 us
  Pallas kernels: 0 us -> 138 us
  blocking collectives: 87.7 us -> 0 us
  matrix products: 21.2 us -> 0 us
  between operations: 17.1 us -> 0.65 us
  other arithmetic: 10.1 us -> 3.7 us
  local copies, waits for them, and re-layouts: 14 us -> 7.79 us
  starting transfers between devices: 4.72 us -> 0 us
    reduce_scatter x1 -> x0, waiting for transfers between devices: 218 us -> none  [per_device(): lax.psum_scatter(local_grads, 'shard', scatter_dimension=1, tiled=True)]
    pallas_call x0 -> x1, Pallas kernels: none -> 138 us  [fused(): pl.pallas_call(fused_kernel, out_shape=(shape(weights.shape, F32), shape(...]
    all_to_all x1 -> x0, blocking collectives: 53.4 us -> none  [per_device(): lax.all_to_all(buffer, ('shard', 'tensor'), split_axis=0, concat_axis=0,...]
    psum x1 -> x0, blocking collectives: 34.3 us -> none  [per_device(): ln_gradient = lax.psum(local_norms, 'shard')]
    dot_general x8 -> x0, matrix products: 21.2 us -> none  [the longest x2 6.95 us: slot_step(): jnp.dot(root_lhs, gradient, precision=PRECISE)]
    scatter x1 -> x0, local copies, waits for them, and re-layouts: 7.15 us -> none  [per_device(): buffer = buffer.at[owner_device, slot_place].set(row_part)]
    unnamed x22 -> x13, local copies, waits for them, and re-layouts: 1.09 us -> 7.79 us
    all_to_all x1 -> x0, starting transfers between devices: 4.68 us -> none  [per_device(): lax.all_to_all(outgoing, ('shard', 'tensor'), split_axis=0, concat_axis=0...]
  transfers between devices with their start and end apart: 2 -> 0, of which waited for: 1 -> 0; matrix products, arithmetic and copies ran while one was open for 3% -> 0% of each run, Pallas kernels for 0% -> 0%
where the time goes in v1:
time: 151 us; the launch traced here: 150 us
  Pallas kernels  138 us (91%)
  local copies, waits for them, and re-layouts  7.79 us (5%)
  other arithmetic  3.7 us (2%)
    pallas_call x1, Pallas kernels, fused(): pl.pallas_call(fused_kernel, out_shape=(shape(weights.shape, F32), shape(...  138 us
    unnamed x13, local copies, waits for them, and re-layouts  7.79 us

profile of v1, /device:TPU:8, one launch (start us, length us, event | category | flops | bytes accessed | tf_op | source)
XLA Modules:
  0.0 149.8 jit_solution(622295939910283938)
XLA Ops:
  0.6 1.3 select_reduce_fusion.block_of
  1.9 1.2 fusion.2.place_of
  3.1 0.7 fusion
  3.8 0.5 convert_element_type.3.filled
  4.3 137.7 %shard_map.137 = (f32[50,64,128]{2,1,0:T(8,128)}, f32[2,512,512]{2,1,0:T(8,128)}, f32[2,512,512]{2,1,0:T(8,128)}, f32[4,256]{1,0:T(4,128)}, f32[4,256]{1,0:T(4,128)}) custom-call(s32[64]{0:T(128)} %select_reduce_fusion.block_of, f32[64]{0:T(128)} %convert_element_type.3.filled, s32[50]{0:T(128)} %fusion.2.place_of, f32[50,512,128]{2,1,0:T(8,128)} %bitcast.2, ...), custom_call_target="tpu_custom_call" | custom-call | flops 17179869184 | bytes 33554432 | tf_op jit(solution)/shard_map/pallas_call | solution.py:328
  142.0 0.0 copy-start.1
  142.0 2.9 %copy.20 = f32[50,64,128]{2,1,0:T(8,128)} copy(f32[50,64,128]{2,1,0:T(8,128)} %get-tuple-element.10) | data formatting | bytes 3276800
  145.0 0.0 copy-done.1
  145.0 0.0 copy-start
  145.0 1.3 copy.21
  146.3 1.0 copy-done
  147.3 0.0 copy-start.3
  147.3 0.0 copy-start.2
  147.3 1.3 copy.22
  148.6 0.0 copy-done.3
  148.7 0.6 copy.23
  149.2 0.0 copy-done.2
  149.2 0.6 copy.24
Async XLA Ops:
  142.0 2.9 %copy-start.1 = (f32[2,512,512]{2,1,0:T(8,128)S(1)}, f32[2,512,512]{2,1,0:T(8,128)}, u32[]{:S(2)}) copy-start(f32[2,512,512]{2,1,0:T(8,128)} %get-tuple-element.11) | copy-start | bytes 6291460
  145.0 2.3 %copy-start = (f32[2,512,512]{2,1,0:T(8,128)S(1)}, f32[2,512,512]{2,1,0:T(8,128)}, u32[]{:S(2)}) copy-start(f32[2,512,512]{2,1,0:T(8,128)} %get-tuple-element.12) | copy-start | bytes 6291460
  147.3 1.3 copy-start.3
  147.3 1.9 %copy-start.2 = (f32[4,256]{1,0:T(4,128)S(1)}, f32[4,256]{1,0:T(4,128)}, u32[]{:S(2)}) copy-start(f32[4,256]{1,0:T(4,128)} %get-tuple-element.14) | copy-start | bytes 12292

commit v2 on v1

--- a/solution.py
+++ b/solution.py
@@ -28,12 +28,11 @@
 
 
 def fused_kernel(
-    block_of, filled, place_of,
-    grad_hbm, weights_ref, stat_l_hbm, stat_r_hbm, root_l_hbm, root_r_hbm, ln_part, ln_params, ln_accum,
-    new_w, new_l_hbm, new_r_hbm, new_lnp, new_lna,
-    grad, ysend, yrecv, zup, zdown, zsend, total, final, gather, stat_l, stat_r, root_l, root_r,
-    g_high, g_low, r_high, r_low, direct, upd, ret, ln_all,
-    load_sem, out_sem, ys_sem, yr_sem, zs_sem, zu_sem, zd_sem, gs_sem, gr_sem, us_sem, ur_sem, ls_sem, lr_sem,
+    block_of, grad_hbm, root_l_hbm, root_r_hbm, ln_part,
+    ret, g_high, ln_sum,
+    grad, ysend, yrecv, zup, zdown, zsend, final, gather, root_l, root_r,
+    g_low, r_high, r_low, direct, upd, ln_all,
+    load_sem, ys_sem, yr_sem, zs_sem, zu_sem, zd_sem, gs_sem, gr_sem, us_sem, ur_sem, ls_sem, lr_sem,
 ):
     side = grad.shape[1]
     width = grad.shape[2]
@@ -43,6 +42,7 @@
     me = sh * 4 + t
     tile = 128
     tiles = side // tile
+    parts = [slice(k * tile, (k + 1) * tile) for k in range(tiles)]
 
     def load(src, dst, k):
         return pltpu.make_async_copy(src, dst, load_sem.at[k])
@@ -51,8 +51,6 @@
         load(grad_hbm, grad, 0),
         load(root_l_hbm, root_l, 1),
         load(root_r_hbm, root_r, 2),
-        load(stat_l_hbm, stat_l, 3),
-        load(stat_r_hbm, stat_r, 4),
     ]
     for one in loads:
         one.start()
@@ -77,12 +75,20 @@
         return jnp.where(z < 2, one, 3 - one)
 
     def unit(n):
-        c, td = n // 4, lax.rem(n, 4)
-        j, zd = c // 4, level(c)
+        k = jnp.maximum(n - 3, 0)
+        last = (n >= 3) & ((lax.rem(k, 4) == 3) | (k == 28))
+        group = jnp.where(last | (n < 3), k // 4, k // 4 + 1)
+        place = jnp.where(last, 3, jnp.where(n < 3, n, lax.rem(k, 4)))
+        j, zd = group // 4, level(place)
+        td = lax.rem(lax.rem(group, 4) + 1 + t, 4)
         return j, zd, td, (j * 4 + zd) * 4 + td
 
     def slot(j, zd, yd, td):
         return ((zd * 2 + yd) * 4 + td) * 2 + j
+
+    def found(s):
+        block = block_of[s]
+        return jnp.maximum(block, 0), jnp.minimum(block + 1, 1).astype(F32)
 
     def y_copy(u):
         return remote(ysend.at[u], yrecv.at[u], ys_sem.at[u], yr_sem.at[u], z * 2 + (1 - y), t)
@@ -92,14 +98,10 @@
     def send_y(n, _):
         j, zd, td, u = unit(n)
         s = slot(j, zd, 1 - y, td)
-        block, keep = block_of[s], filled[s]
-
-        def rows(i, _):
-            r = pl.ds(pl.multiple_of(i * tile, tile), tile)
+        block, keep = found(s)
+
+        for r in parts:
             ysend[u, r, :] = (grad[block, r, :] * keep).astype(BF16)
-            return 0
-
-        lax.fori_loop(0, tiles, rows, 0)
         y_copy(u).start()
         return 0
 
@@ -116,49 +118,36 @@
 
     def gather_wait(j, tt):
         return remote(final.at[j, tt], gather.at[j, tt], gs_sem.at[j, tt], gr_sem.at[j, tt], sh, tt)
-
-    def each_tile(body):
-        def step(i, _):
-            body(pl.ds(pl.multiple_of(i * tile, tile), tile))
-            return 0
-
-        lax.fori_loop(0, tiles, step, 0)
 
     def reduce_unit(n, _):
         j, zd, td, u = unit(n)
         s = slot(j, zd, y, td)
-        block, keep = block_of[s], filled[s]
+        block, keep = found(s)
         y_copy(u).wait_recv()
 
-        def first(r):
-            total[r, :] = grad[block, r, :] * keep + yrecv[u, r, :].astype(F32)
-
-        each_tile(first)
-
-        @pl.when((z > 0) & (zd >= z))
+        def summed(r, *more):
+            value = grad[block, r, :] * keep + yrecv[u, r, :].astype(F32)
+            for one in more:
+                value = value + one[u, r, :].astype(F32)
+            return value
+
+        def pass_on(*more):
+            for r in parts:
+                zsend[u, r, :] = summed(r, *more).astype(BF16)
+
+        @pl.when(((z == 0) & (zd > 0)) | ((z == 3) & (zd < 3)))
+        def _():
+            pass_on()
+
+        @pl.when((zd > z) & (z > 0))
         def _():
             up_copy(u).wait_recv()
-
-            def add(r):
-                total[r, :] = total[r, :] + zup[u, r, :].astype(F32)
-
-            each_tile(add)
-
-        @pl.when((z < 3) & (zd <= z))
+            pass_on(zup)
+
+        @pl.when((zd < z) & (z < 3))
         def _():
             down_copy(u).wait_recv()
-
-            def add(r):
-                total[r, :] = total[r, :] + zdown[u, r, :].astype(F32)
-
-            each_tile(add)
-
-        @pl.when(zd != z)
-        def _():
-            def narrow(r):
-                zsend[u, r, :] = total[r, :].astype(BF16)
-
-            each_tile(narrow)
+            pass_on(zdown)
 
         @pl.when(zd > z)
         def _():
@@ -168,20 +157,34 @@
         def _():
             down_copy(u).start()
 
+        def finish(*more):
+            for r in parts:
+                final[j, td, r, :] = summed(r, *more)
+
+        @pl.when((zd == z) & (z == 0))
+        def _():
+            down_copy(u).wait_recv()
+            finish(zdown)
+
+        @pl.when((zd == z) & (z == 3))
+        def _():
+            up_copy(u).wait_recv()
+            finish(zup)
+
+        @pl.when((zd == z) & (z > 0) & (z < 3))
+        def _():
+            up_copy(u).wait_recv()
+            down_copy(u).wait_recv()
+            finish(zup, zdown)
+
         @pl.when((zd == z) & (td != t))
         def _():
-            def keep_sum(r):
-                final[j, td, r, :] = total[r, :]
-
-            each_tile(keep_sum)
             gather_copy(j, td).start()
 
         @pl.when((zd == z) & (td == t))
         def _():
-            def keep_own(r):
-                gather[j, t, r, :] = total[r, :]
-
-            each_tile(keep_own)
+            for r in parts:
+                gather[j, t, r, :] = final[j, td, r, :]
 
         return 0
 
@@ -196,36 +199,30 @@
             gather_wait(j, lax.rem(t + k, 4)).wait_recv()
         cols = [slice(k * width, (k + 1) * width) for k in range(4)]
 
-        def halves(i, sq):
-            r = pl.ds(pl.multiple_of(i * tile, tile), tile)
+        sq = jnp.zeros((1, width), F32)
+        for r in parts:
             for k in range(4):
                 g = gather[j, k, r, :]
                 sq = sq + jnp.sum(g * g, axis=0, keepdims=True)
                 g_high[j, r, cols[k]], g_low[r, cols[k]] = split(g)
-            r_high[r, :], r_low[r, :] = split(root_r[j, r, :])
-            return sq
-
-        zero = jnp.zeros((1, width), F32)
-        square = jnp.sum(lax.fori_loop(0, tiles, halves, zero)) * (1.0 / (side * side))
+        square = jnp.sum(sq) * (1.0 / (side * side))
 
         def product(i, sq):
-            r = pl.ds(pl.multiple_of(i * tile, tile), tile)
+            r = pl.ds(pl.multiple_of(i * 256, 256), 256)
             half = mul3(*split(root_l[j, r, :]), g_high[j], g_low[...])
-            out = mul3(*split(half), r_high[...], r_low[...])
+            out = mul3(*split(half), r_high[j], r_low[j])
             direct[r, :] = out
             for k in range(4):
                 sq = sq + jnp.sum(out[:, cols[k]] * out[:, cols[k]], axis=0, keepdims=True)
             return sq
 
-        mean = jnp.sum(lax.fori_loop(0, tiles, product, zero)) * (1.0 / (side * side))
+        sq = lax.fori_loop(0, side // 256, product, jnp.zeros((1, width), F32))
+        mean = jnp.sum(sq) * (1.0 / (side * side))
         ratio = jnp.full((1, width), square, F32) / (jnp.full((1, width), mean, F32) + EPSILON)
         scale = STEP_RATE * jnp.sqrt(ratio)
-
-        def scaled(r):
+        for r in parts:
             for k in range(4):
                 upd[j, k, r, :] = (direct[r, cols[k]] * scale).astype(BF16)
-
-        each_tile(scaled)
         own = pl.ds(pl.multiple_of(sh * 64, 64), 64)
         ret[j * 32 + me] = upd[j, t, own, :]
 
@@ -235,40 +232,20 @@
 
         lax.fori_loop(1, 32, start, 0)
 
-    def statistics(j):
-        def left(i, _):
-            r = pl.ds(pl.multiple_of(i * tile, tile), tile)
-            square = lax.dot_general(
-                g_high[j, r, :], g_high[j], (((1,), (1,)), ((), ())), preferred_element_type=F32
-            )
-            stat_l[j, r, :] = DECAY_RATE * stat_l[j, r, :] + (1.0 - DECAY_RATE) * square
-            return 0
-
-        lax.fori_loop(0, tiles, left, 0)
-
-        def right(k, _):
-            r = pl.ds(pl.multiple_of(k * width, width), width)
-            flipped = gather[j, k].T.astype(BF16)
-            stat_r[j, r, :] = DECAY_RATE * stat_r[j, r, :] + (1.0 - DECAY_RATE) * mul(flipped, g_high[j])
-            return 0
-
-        lax.fori_loop(0, 4, right, 0)
-
-    lax.fori_loop(0, 20, reduce_unit, 0)
     loads[1].wait()
     loads[2].wait()
+
+    def split_right(i, _):
+        r = pl.ds(pl.multiple_of(i * tile, tile), tile)
+        for j in range(2):
+            r_high[j, r, :], r_low[j, r, :] = split(root_r[j, r, :])
+        return 0
+
+    lax.fori_loop(0, tiles, split_right, 0)
+    lax.fori_loop(0, 22, reduce_unit, 0)
     precondition(0)
-    lax.fori_loop(20, 32, reduce_unit, 0)
+    lax.fori_loop(22, 32, reduce_unit, 0)
     precondition(1)
-
-    loads[3].wait()
-    loads[4].wait()
-    statistics(0)
-    statistics(1)
-    out_l = pltpu.make_async_copy(stat_l, new_l_hbm, out_sem.at[0])
-    out_r = pltpu.make_async_copy(stat_r, new_r_hbm, out_sem.at[1])
-    out_l.start()
-    out_r.start()
 
     for k in range(1, 8):
         ln_copy(k).wait()
@@ -276,9 +253,7 @@
     ln_grad = ln_all[0]
     for k in range(1, 8):
         ln_grad = ln_grad + ln_all[k]
-    accum = ln_accum[...] + ln_grad * ln_grad
-    new_lna[...] = accum
-    new_lnp[...] = ln_params[...] - NORM_RATE * ln_grad / jnp.sqrt(accum)
+    ln_sum[...] = ln_grad
 
     def sent(n, _):
         _, zd, _, u = unit(n)
@@ -301,22 +276,55 @@
 
     lax.fori_loop(0, 62, landed, 0)
 
-    def apply(k, _):
-        new_w[k] = weights_ref[k] - ret[place_of[k]].astype(F32)
-        return 0
-
-    lax.fori_loop(0, weights_ref.shape[0], apply, 0)
-    out_l.wait()
-    out_r.wait()
+
+def closing_kernel(
+    owner_slot, pieces, grads, weights, stat_l, stat_r, ln_grad, ln_params, ln_accum,
+    new_w, new_l, new_r, new_lnp, new_lna,
+):
+    step = pl.program_id(0)
+    accum = ln_accum[...] + ln_grad[...] * ln_grad[...]
+    new_lna[...] = accum
+    new_lnp[...] = ln_params[...] - NORM_RATE * ln_grad[...] / jnp.sqrt(accum)
+    tile = stat_l.shape[1]
+    first = step * weights.shape[0]
+    count = owner_slot.shape[0]
+    for k in range(weights.shape[0]):
+        s = owner_slot[jnp.minimum(first + k, count - 1)]
+        new_w[k] = weights[k] - pieces[lax.rem(s, 2) * 32 + s // 2].astype(F32)
+    at = pl.ds(pl.multiple_of(lax.rem(step, grads.shape[1] // tile) * tile, tile), tile)
+    square = lax.dot_general(grads[0, at, :], grads[0], (((1,), (1,)), ((), ())), preferred_element_type=F32)
+    new_l[0] = DECAY_RATE * stat_l[0] + (1.0 - DECAY_RATE) * square
+    flipped = grads[0, :, at].astype(F32).T.astype(BF16)
+    new_r[0] = DECAY_RATE * stat_r[0] + (1.0 - DECAY_RATE) * mul(flipped, grads[0])
+
+
+def closing(owner_slot, pieces, grads, weights, stat_left, stat_right, ln_grad, ln_params, ln_accum):
+    side = stat_left.shape[1]
+    rows = 4
+    steps = 2 * rows
+    some = pl.BlockSpec((-(-weights.shape[0] // steps),) + weights.shape[1:], lambda i: (i, 0, 0))
+    norm = pl.BlockSpec(ln_params.shape, lambda i: (0, 0))
+    stat = pl.BlockSpec((1, side // rows, side), lambda i: (i // rows, i % rows, 0))
+    return pl.pallas_call(
+        closing_kernel,
+        grid=(steps,),
+        out_shape=tuple(jax.ShapeDtypeStruct(v.shape, F32) for v in (weights, stat_left, stat_right, ln_params, ln_accum)),
+        in_specs=[
+            pl.BlockSpec(memory_space=pltpu.SMEM),
+            pl.BlockSpec(pieces.shape, lambda i: (0, 0, 0)),
+            pl.BlockSpec((1, side, side), lambda i: (i // rows, 0, 0)),
+            some, stat, stat, norm, norm, norm,
+        ],
+        out_specs=(some, stat, stat, norm, norm),
+        compiler_params=pltpu.CompilerParams(vmem_limit_bytes=60 * 2**20),
+    )(owner_slot, pieces, grads, weights, stat_left, stat_right, ln_grad, ln_params, ln_accum)
 
 
 def fused(grad_parts, weights, owner_slot, stat_left, stat_right, root_left, root_right, ln_grad_parts, ln_params, ln_accum):
     blocks, side, width = grad_parts.shape[1:]
     slots = 64
     hit = owner_slot[None, :] == jnp.arange(slots, dtype=jnp.int32)[:, None]
-    block_of = jnp.sum(jnp.where(hit, jnp.arange(blocks, dtype=jnp.int32)[None, :], 0), axis=1).astype(jnp.int32)
-    filled = jnp.any(hit, axis=1).astype(F32)
-    place_of = (owner_slot % 2) * 32 + owner_slot // 2
+    block_of = jnp.max(jnp.where(hit, jnp.arange(blocks, dtype=jnp.int32)[None, :], -1), axis=1)
     smem = pl.BlockSpec(memory_space=pltpu.SMEM)
     vmem = pl.BlockSpec(memory_space=pltpu.VMEM)
     hbm = pl.BlockSpec(memory_space=pl.ANY)
@@ -325,26 +333,24 @@
     unit = (32, side, width)
     state = (2, side, side)
     shape = jax.ShapeDtypeStruct
-    return pl.pallas_call(
+    pieces, grads, ln_grad = pl.pallas_call(
         fused_kernel,
         out_shape=(
-            shape(weights.shape, F32), shape(state, F32), shape(state, F32),
-            shape(ln_params.shape, F32), shape(ln_params.shape, F32),
+            shape((64, 64, width), BF16), shape(state, BF16),
+            shape(ln_params.shape, F32),
         ),
-        in_specs=[smem] * 3 + [hbm, vmem] + [hbm] * 4 + [vmem] * 3,
-        out_specs=(vmem, hbm, hbm, vmem, vmem),
+        in_specs=[smem] + [hbm] * 3 + [vmem],
+        out_specs=(vmem,) * 3,
         scratch_shapes=[
             V((blocks, side, width), F32),
             V(unit, BF16), V(unit, BF16), V(unit, BF16), V(unit, BF16), V(unit, BF16),
-            V((side, width), F32),
             V((2, 4, side, width), F32), V((2, 4, side, width), F32),
-            V(state, F32), V(state, F32), V(state, F32), V(state, F32),
-            V(state, BF16), V((side, side), BF16), V((side, side), BF16), V((side, side), BF16),
+            V(state, F32), V(state, F32),
+            V((side, side), BF16), V(state, BF16), V(state, BF16),
             V((side, side), F32),
             V((2, 4, side, width), BF16),
-            V((64, 64, width), BF16),
             V((8,) + ln_params.shape, F32),
-            dma((5,)), dma((2,)),
+            dma((3,)),
             dma((32,)), dma((32,)), dma((32,)), dma((32,)), dma((32,)),
             dma((2, 4)), dma((2, 4)),
             dma((2, 31)), dma((2, 31)),
@@ -355,9 +361,10 @@
         ),
         cost_estimate=pl.CostEstimate(flops=2**34, bytes_accessed=2**25, transcendentals=0),
     )(
-        block_of, filled, place_of,
-        grad_parts[0], weights, stat_left, stat_right, root_left, root_right,
-        ln_grad_parts[0], ln_params, ln_accum,
+        block_of, grad_parts[0], root_left, root_right, ln_grad_parts[0],
+    )
+    return closing(
+        owner_slot, pieces, grads, weights, stat_left, stat_right, ln_grad, ln_params, ln_accum
     )
 
 

time: 151 us -> 144 us (0.954)
  local copies, waits for them, and re-layouts: 7.79 us -> 0 us
  other arithmetic: 3.7 us -> 1.26 us
    unnamed x13 -> x0, local copies, waits for them, and re-layouts: 7.79 us -> none
    pallas_call x1 -> x2, Pallas kernels: 138 us -> 139 us  [the longest x1 130 us: fused(): pl.pallas_call(fused_kernel, out_shape=(shape((64, 64, width), BF16), sha...]
where the time goes in v2:
time: 144 us; the launch traced here: 141 us
  Pallas kernels  139 us (97%)
    pallas_call x1, Pallas kernels, fused(): pl.pallas_call(fused_kernel, out_shape=(shape((64, 64, width), BF16), sha...  130 us
    pallas_call x1, Pallas kernels, closing(): pl.pallas_call(closing_kernel, grid=(steps,), out_shape=tuple((jax.ShapeD...  9.44 us

profile of v2, /device:TPU:8, one launch (start us, length us, event | category | flops | bytes accessed | tf_op | source)
XLA Modules:
  0.0 141.3 jit_solution(2523758549104963509)
XLA Ops:
  0.6 1.3 select_reduce_fusion.block_of
  1.9 130.0 %shard_map.137 = (bf16[64,64,128]{2,1,0:T(8,128)(2,1)}, bf16[2,512,512]{2,1,0:T(8,128)(2,1)}, f32[4,256]{1,0:T(4,128)}) custom-call(s32[64]{0:T(128)} %select_reduce_fusion.block_of, f32[50,512,128]{2,1,0:T(8,128)} %bitcast.2, f32[2,512,512]{2,1,0:T(8,128)} %root_l_hbm.1, f32[2,512,512]{2,1,0:T(8,128)} %root_r_hbm.1, f32[4,256]{1,0:T(4,128)} %bitcast.3), custom_call_target="tpu_custom_call" | custom-call | flops 17179869184 | bytes 33554432 | tf_op jit(solution)/shard_map/pallas_call | solution.py:336
  131.9 9.4 %shard_map.138 = (f32[50,64,128]{2,1,0:T(8,128)}, f32[2,512,512]{2,1,0:T(8,128)}, f32[2,512,512]{2,1,0:T(8,128)}, f32[4,256]{1,0:T(4,128)}, f32[4,256]{1,0:T(4,128)}) custom-call(s32[50]{0:T(128)} %owner_slot.1, bf16[64,64,128]{2,1,0:T(8,128)(2,1)} %get-tuple-element.8.pieces, bf16[2,512,512]{2,1,0:T(8,128)(2,1)} %get-tuple-element.9.grads, ...), custom_call_target="tpu_custom_call" | custom-call | tf_op jit(solution)/shard_map/pallas_call | solution.py:308
